TPU v7x, 32 devices: a whole 2x2x4 slice. The times are simulated.
32 devices in a mesh: tsink: 4 (over y, x), mom: 8 (over z, core).
Axes of the slice: x: 2, y: 2, z: 4, core: 2. Of those that a mesh axis runs over, the one named last changes fastest.
Arguments:
- perambulators: bfloat16 [4, 4, 1024, 1024], P('tsink'), may hold values from -0.1875 to 0.1875
- elementals: bfloat16 [4, 8, 1024, 1024], P('tsink', 'mom'), may hold values from -6 to 6
- src_times: int32 [4], replicated, may hold values from 0 to 3, as said below
- diagrams: int32 [64, 2], replicated, may hold values from 0 to 7
Outputs:
- meson_blocks: bfloat16 [4, 8, 1024, 1024], P('tsink', 'mom')
- correlators: float32 [64, 4], P('mom', 'tsink')
Inputs may be any that keep to these rules, and one draw needn't show every extreme that they name: `src_times`: distinct time slices; the first and the last time slice are always among them.
All inputs are finite; a program needn't handle non-finite values.
Results may differ from a plain program's by a relative error of at most 0.0055.
Values may be sent and summed in bfloat16 or wider, within the bound.
A program may use at most 192 MiB of HBM per device.

v0:
```python
import jax
import jax.numpy as jnp
from jax import lax
from jax.sharding import PartitionSpec as P

NSRC = 4


def from_root(block, axis, source):
    block = jnp.where(lax.axis_index(axis) == source, block, jnp.zeros_like(block))
    return lax.psum(block, axis)


def body(perambulators, elementals, src_times, diagrams):
    propagators = perambulators[0]
    own_elemental = elementals[0, 0]
    block_order = propagators.shape[1]
    summed = jnp.zeros((block_order, block_order), jnp.float32)
    for source in range(NSRC):
        elemental = from_root(own_elemental, "tsink", src_times[source])
        half_product = lax.dot_general(
            elemental,
            propagators[source],
            (((1,), (1,)), ((), ())),
            preferred_element_type=jnp.float32,
        ).astype(jnp.bfloat16)
        summed = summed + jnp.dot(
            propagators[source], half_product, preferred_element_type=jnp.float32
        )
    meson = summed.astype(jnp.bfloat16)
    gathered = lax.all_gather(meson[None], "mom", axis=0, tiled=True)
    per_device = diagrams.shape[0] // lax.axis_size("mom")
    own_diagrams = lax.dynamic_slice_in_dim(
        diagrams, lax.axis_index("mom") * per_device, per_device, 0
    )

    def whole_trace(diagram_pair):
        return (
            jnp.einsum(
                "ij,ji->",
                gathered[diagram_pair[0]],
                gathered[diagram_pair[1]],
                preferred_element_type=jnp.float32,
            )
            / block_order
        )

    traces = lax.map(whole_trace, own_diagrams)
    correlators = traces[:, None]
    return (meson[None, None], correlators)


def solution(mesh):
    in_specs = (P("tsink", None, None, None), P("tsink", "mom", None, None), P(), P())
    out_specs = (P("tsink", "mom", None, None), P("mom", "tsink"))
    return jax.shard_map(body, mesh=mesh, in_specs=in_specs, out_specs=out_specs, check_vma=False)
```

profile of v0, /device:TPU:0, one launch (start us, length us, event | category | flops | bytes accessed | tf_op | source)
XLA Modules:
  0.0 566.4 jit_solution(11608092730399147223)
XLA Ops:
  7.2 1.4 fusion.51
  11.2 5.1 select_bitcast_fusion.3
  16.3 0.0 all-gather.3.cloned.1.call-start
  16.3 176.5 %all-reduce.3.cloned.1.call-done = (bf16[1024,1024]{1,0:T(8,128)(2,1)}, bf16[1024,1024]{1,0:T(8,128)(2,1)}, bf16[1024,1024]{1,0:T(8,128)(2,1)}, bf16[1024,1024]{1,0:T(8,128)(2,1)}) async-done(((bf16[1024,1024]{1,0:T(8,128)(2,1)}, bf16[1024,1024]{1,0:T(8,128)(2,1)}, bf16[1024,1024]{1,0:T(8,128)(2,1)}, bf16[1024,1024]{1,0:T(8,128)(2,1)}), (bf16[1024,1024]{1,0:T(8,128)(2,1)}, bf16[1024,1024]{1,0:T(8,128)(2,1)}, ...) | async-done | bytes 8388624 | tf_op jit(solution)/shard_map/psum | solution.py:11
  192.8 9.5 %fusion = f32[1024,1024]{1,0:T(8,128)} fusion(bf16[1,4,1024,1024]{3,2,1,0:T(8,128)(2,1)} %param.6, bf16[1024,1024]{1,0:T(8,128)(2,1)} %get-tuple-element.39), kind=kOutput, calls=%fused_computation.4 | convolution fusion | flops 4296015872 | bytes 10485760 | tf_op jit(solution)/shard_map/dot_general | solution.py:27
  202.3 8.7 %fusion.4 = f32[1024,1024]{1,0:T(8,128)} fusion(bf16[1,4,1024,1024]{3,2,1,0:T(8,128)(2,1)} %param.6, bf16[1024,1024]{1,0:T(8,128)(2,1)S(1)} %copy-done.4), kind=kOutput, calls=%fused_computation.8 | convolution fusion | flops 4296015872 | bytes 10485760 | tf_op jit(solution)/shard_map/dot_general | solution.py:27
  211.0 9.7 %fusion.8 = f32[1024,1024]{1,0:T(8,128)} fusion(bf16[1,4,1024,1024]{3,2,1,0:T(8,128)(2,1)} %param.6, bf16[1024,1024]{1,0:T(8,128)(2,1)} %get-tuple-element.41), kind=kOutput, calls=%fused_computation.12 | convolution fusion | flops 4296015872 | bytes 10485760 | tf_op jit(solution)/shard_map/dot_general | solution.py:27
  220.7 11.6 %add_convert_fusion = bf16[1024,1024]{1,0:T(8,128)(2,1)} fusion(f32[1024,1024]{1,0:T(8,128)} %fusion, f32[1024,1024]{1,0:T(8,128)} %fusion.4, f32[1024,1024]{1,0:T(8,128)} %fusion.8, bf16[1,4,1024,1024]{3,2,1,0:T(8,128)(2,1)} %param.6, bf16[1024,1024]{1,0:T(8,128)(2,1)S(1)} %copy-done.3), kind=kOutput, calls=%fused_computation.3 | convolution fusion | flops 4300210176 | bytes 20971520 | tf_op jit(solution)/shard_map/dot_general | solution.py:27
  232.4 0.1 constant_dynamic-slice_fusion.1
  232.4 1.5 copy-done.2
  233.9 2.5 copy.7
  236.4 147.9 %all-gather.3.cloned.1.call-done = bf16[8192,1024]{0,1:T(8,128)(2,1)} async-done(((bf16[1024,1024]{0,1:T(8,128)(2,1)}), bf16[8192,1024]{0,1:T(8,128)(2,1)}) %all-gather.3.cloned.1.call-update) | async-done | bytes 16777232 | tf_op jit(solution)/shard_map/all_gather | solution.py:31
  384.3 22.3 %copy.13 = bf16[8192,1024]{1,0:T(8,128)(2,1)} copy(bf16[8192,1024]{0,1:T(8,128)(2,1)} %all-gather.3.cloned.1.call-done) | data formatting | bytes 33554432 | tf_op jit(solution)/shard_map/while | solution.py:48
  406.6 152.3 %while.10 = (s32[]{:T(128)}, f32[8]{0:T(128)S(1)}, s32[8,2]{0,1:T(2,128)S(1)}, bf16[8,1024,1024]{2,1,0:T(8,128)(2,1)}, s32[]{:T(128)}, /*index=5*/s32[]{:T(128)}, s32[]{:T(128)}, f32[]{:T(128)}) while((s32[]{:T(128)}, f32[8]{0:T(128)S(1)}, s32[8,2]{0,1:T(2,128)S(1)}, bf16[8,1024,1024]{2,1,0:T(8,128)(2,1)}, s32[]{:T(128)}, ...), condition=%wide.region_5.6_spmd, body=%wide.region_4.5_spmd.sunk | while | flops 4194312 | bytes 20971744 | solution.py:48
  406.6 0.1 constant_dynamic-slice_fusion.3
  406.7 0.6 fusion.57
  409.2 4.0 bitcast_convert_fusion.2
  413.2 5.4 copy.15
  420.3 4.6 multiply_reduce_fusion.2
  425.6 0.1 dynamic_update_slice.5
  425.7 0.1 constant_dynamic-slice_fusion.3
  425.7 0.6 fusion.57
  428.2 4.0 bitcast_convert_fusion.2
  432.2 5.4 copy.15
  439.3 4.6 multiply_reduce_fusion.2
  444.6 0.1 dynamic_update_slice.5
  444.7 0.1 constant_dynamic-slice_fusion.3
  444.8 0.6 fusion.57
  447.3 4.0 bitcast_convert_fusion.2
  451.3 5.4 copy.15
  458.3 4.6 multiply_reduce_fusion.2
  463.6 0.1 dynamic_update_slice.5
  463.7 0.1 constant_dynamic-slice_fusion.3
  463.8 0.6 fusion.57
  466.3 4.0 bitcast_convert_fusion.2
  470.3 5.4 copy.15
  477.4 4.6 multiply_reduce_fusion.2
  482.7 0.1 dynamic_update_slice.5
  482.8 0.1 constant_dynamic-slice_fusion.3
  482.8 0.6 fusion.57
  485.3 4.0 bitcast_convert_fusion.2
  489.3 5.4 copy.15
  496.4 4.6 multiply_reduce_fusion.2
  501.7 0.1 dynamic_update_slice.5
  501.8 0.1 constant_dynamic-slice_fusion.3
  501.9 0.6 fusion.57
  504.4 4.0 bitcast_convert_fusion.2
  508.4 5.4 copy.15
  515.4 4.6 multiply_reduce_fusion.2
  520.7 0.1 dynamic_update_slice.5
  520.8 0.1 constant_dynamic-slice_fusion.3
  520.9 0.6 fusion.57
  523.4 4.0 bitcast_convert_fusion.2
  527.4 5.4 copy.15
  534.5 4.6 multiply_reduce_fusion.2
  539.8 0.1 dynamic_update_slice.5
  539.9 0.1 constant_dynamic-slice_fusion.3
  540.0 0.6 fusion.57
  542.4 4.0 bitcast_convert_fusion.2
  546.5 5.4 copy.15
  553.5 4.6 multiply_reduce_fusion.2
  558.8 0.1 dynamic_update_slice.5
  558.9 0.5 copy-done.5
  559.4 0.2 copy-done.1
  (13 shorter events, 0.1 us)
Async XLA Ops:
  7.2 225.2 %copy-start = (s32[64,2]{0,1:T(2,128)S(1)}, s32[64,2]{0,1:T(2,128)}, u32[]{:S(2)}) copy-start(s32[64,2]{0,1:T(2,128)} %param.9) | copy-start | bytes 1540
  7.2 185.6 %all-reduce.3.cloned.1.call-start = ((), (), s32[]{:S(2)}) async-start(), calls=%async_computation.1 | async-start | bytes 16777216 | tf_op jit(solution)/shard_map/psum | solution.py:11
  16.3 368.0 %all-gather.3.cloned.1.call-start = ((), (), s32[]{:S(2)}) async-start(), calls=%async_computation | async-start | bytes 18874368 | tf_op jit(solution)/shard_map/all_gather | solution.py:31
  192.8 9.5 %copy-start.4 = (bf16[1024,1024]{1,0:T(8,128)(2,1)S(1)}, bf16[1024,1024]{1,0:T(8,128)(2,1)}, u32[]{:S(2)}) copy-start(bf16[1024,1024]{1,0:T(8,128)(2,1)} %get-tuple-element.40) | copy-start | bytes 6291460
  211.0 9.7 %copy-start.3 = (bf16[1024,1024]{1,0:T(8,128)(2,1)S(1)}, bf16[1024,1024]{1,0:T(8,128)(2,1)}, u32[]{:S(2)}) copy-start(bf16[1024,1024]{1,0:T(8,128)(2,1)} %get-tuple-element.42) | copy-start | bytes 6291460
  232.3 1.6 copy-start.2
  558.9 0.5 copy-start.5
  558.9 0.7 copy-start.1
Sparse Core Ops, SparseCore 0:
  16.4 176.3 all-reduce.2
  232.5 151.7 all-gather.2
where the time goes:
time: 568 us; the launch traced here: 566 us
  waiting for transfers between devices  324 us (57%)
  local copies, waits for them, and re-layouts  77.6 us (14%)
  other arithmetic  74.2 us (13%)
  matrix products  39.5 us (7%)
  loops' own time  34.1 us (6%)
  between operations  16.6 us (3%)
    psum x1, waiting for transfers between devices, from_root(): return lax.psum(block, axis)  176 us
    all_gather x1, waiting for transfers between devices, body(): gathered = lax.all_gather(meson[None], 'mom', axis=0, tiled=True)  148 us
    while x8, local copies, waits for them, and re-layouts  42.9 us
    dot_general x4, matrix products, body(): jnp.dot(propagators[source], half_product, preferred_element_type=jnp.flo...  39.5 us
    dot_general x8, other arithmetic, whole_trace(): jnp.einsum('ij,ji->', gathered[diagram_pair[0]], gathered[diagram_pair[1]...  36.9 us
    another operation x1, loops' own time, body(): traces = lax.map(whole_trace, own_diagrams)  34.1 us
    while x8, other arithmetic  32.2 us
    while x1, local copies, waits for them, and re-layouts, body(): traces = lax.map(whole_trace, own_diagrams)  22.3 us
  transfers between devices with their start and end apart: 2, of which 2 were waited for; matrix products, arithmetic and copies ran while one was open for 0% of the time, Pallas kernels for 0%

commit v1 on v0

v1 whole, which is shorter than its diff:
```python
import functools

import jax
import jax.numpy as jnp
from jax import lax
from jax.experimental import pallas as pl
from jax.experimental.pallas import tpu as pltpu
from jax.sharding import PartitionSpec as P

LANES = 128
CHUNK = 256
BF16 = jnp.bfloat16
F32 = jnp.float32


def partner_of(index, mask, size):
    out, digit = 0, 1
    while digit < size:
        mine = lax.rem(lax.div(index, digit), 2)
        if isinstance(mask, int):
            other = (mask // digit) % 2
        else:
            other = lax.rem(lax.div(mask, digit), 2)
        out = out + digit * lax.rem(mine + other, 2)
        digit *= 2
    return out


def kernel(
    n_t, n_mom, n_src, classes, diag_count,
    src_ref, diag_ref, p_hbm, e_hbm,
    out_hbm, corr_ref,
    p, e, acc, half, meson, outbox, inbox, turned, grid, grids,
    p_sem, e_send, e_fwd, e_recv, out_sem, m_send, m_recv, g_send, g_recv,
):
    order = p.shape[1]
    n_chunk = order // CHUNK
    t = lax.axis_index("tsink")
    me = lax.axis_index("mom")

    def rows(c):
        return pl.ds(pl.multiple_of(c * CHUNK, CHUNK), CHUNK)

    p_copies = [
        pltpu.make_async_copy(p_hbm.at[s], p.at[s], p_sem.at[s]) for s in range(n_src)
    ]
    own_copies = [
        pltpu.make_async_copy(
            e_hbm.at[pl.ds(c * CHUNK, CHUNK)], e.at[0, pl.ds(c * CHUNK, CHUNK)], e_recv.at[0, c]
        )
        for c in range(n_chunk)
    ]
    for copy in p_copies + own_copies:
        copy.start()

    barrier = pltpu.get_barrier_semaphore()
    for m in range(1, n_t):
        pl.semaphore_signal(
            barrier, inc=1, device_id={"tsink": partner_of(t, m, n_t)},
            device_id_type=pl.DeviceIdType.MESH,
        )
    for m in range(1, n_mom):
        pl.semaphore_signal(
            barrier, inc=1, device_id={"mom": partner_of(me, m, n_mom)},
            device_id_type=pl.DeviceIdType.MESH,
        )
    pl.semaphore_wait(barrier, n_t - 1 + n_mom - 1)

    square = n_t == 4
    direct = (1, 2) if square else tuple(range(1, n_t))
    sends = []
    for k in range(n_chunk):
        for m in direct:
            c = (k + n_chunk // 2) % n_chunk if square and m == 2 else k
            part = pl.ds(c * CHUNK, CHUNK)
            send = pltpu.make_async_remote_copy(
                src_ref=e_hbm.at[part], dst_ref=e.at[m, part],
                send_sem=e_send.at[m, c], recv_sem=e_recv.at[m, c],
                device_id={"tsink": partner_of(t, m, n_t)},
                device_id_type=pl.DeviceIdType.MESH,
            )
            send.start()
            sends.append(send)

    def forward(slot, c):
        return pltpu.make_async_remote_copy(
            src_ref=e.at[slot, rows(c)], dst_ref=e.at[3, rows(c)],
            send_sem=e_fwd.at[c], recv_sem=e_recv.at[3, c],
            device_id={"tsink": partner_of(t, 3 - slot, n_t)},
            device_id_type=pl.DeviceIdType.MESH,
        )

    def arrived(slot, c):
        pltpu.make_async_copy(e.at[slot, rows(c)], e.at[slot, rows(c)], e_recv.at[slot, c]).wait()

    acc[...] = jnp.zeros_like(acc)
    for copy in p_copies:
        copy.wait()

    def add_chunk(slot, c):
        time = partner_of(t, slot, n_t)
        source = jnp.int32(0)
        weight = jnp.float32(0)
        for s in range(n_src):
            hit = src_ref[s] == time
            source = jnp.where(hit, jnp.int32(s), source)
            weight = jnp.where(hit, jnp.float32(1), weight)
        chunk = e[slot, rows(c), :]

        @pl.loop(0, order // CHUNK)
        def _(n):
            product = lax.dot_general(
                chunk, p[source, rows(n), :], (((1,), (1,)), ((), ())),
                preferred_element_type=F32,
            )
            if n_t > n_src:
                product = product * weight
            half[:, rows(n)] = product.astype(BF16)

        @pl.loop(0, order // CHUNK)
        def _(n):
            acc[rows(n), :] += jnp.dot(
                p[source, rows(n), rows(c)], half[...], preferred_element_type=F32
            )

    @pl.loop(0, n_chunk)
    def _(c):
        arrived(0, c)
        add_chunk(0, c)

    if square:
        @pl.loop(0, 2 * n_chunk)
        def _(k):
            later = lax.rem(k, 2)
            slot = 1 + later
            c = lax.rem(lax.div(k, 2) + later * (n_chunk // 2), n_chunk)
            arrived(slot, c)

            @pl.when(k < n_chunk)
            def _():
                forward(slot, c).start()

            add_chunk(slot, c)

        @pl.loop(0, n_chunk)
        def _(k):
            c = lax.div(k, 2) + lax.rem(k, 2) * (n_chunk // 2)
            arrived(3, c)
            add_chunk(3, c)
    else:
        @pl.loop(n_chunk, n_t * n_chunk)
        def _(k):
            slot, c = lax.div(k, n_chunk), lax.rem(k, n_chunk)
            arrived(slot, c)
            add_chunk(slot, c)

    def strip(i):
        return pl.ds(pl.multiple_of(i * LANES, LANES), LANES)

    @pl.loop(0, classes)
    def _(i):
        values = acc[strip(i), :].astype(BF16)
        meson[strip(i), :] = values
        for j in range(classes):
            outbox[lax.rem(i + j, classes), strip(i), :] = values[:, j * LANES:(j + 1) * LANES]

    def post(m):
        to = partner_of(me, m, n_mom)
        return pltpu.make_async_remote_copy(
            src_ref=outbox.at[lax.rem(to, classes)], dst_ref=inbox.at[m],
            send_sem=m_send.at[m], recv_sem=m_recv.at[m],
            device_id={"mom": to}, device_id_type=pl.DeviceIdType.MESH,
        )

    def if_class(index, action):
        if classes == n_mom:
            action()
        else:
            pl.when(index < classes)(action)

    far_first = sorted(range(1, n_mom), key=lambda m: -(m // (n_mom // 2)))
    for m in far_first:
        if_class(partner_of(me, m, n_mom), lambda: post(m).start())
    out_copy = pltpu.make_async_copy(meson, out_hbm, out_sem)
    out_copy.start()

    row = lax.broadcasted_iota(jnp.int32, grid.shape, 0)
    column = lax.broadcasted_iota(jnp.int32, grid.shape, 1)
    grid[...] = jnp.zeros_like(grid)

    def traces():
        inbox[0] = outbox[lax.rem(me, classes)]

        @pl.loop(0, n_mom)
        def _(m):
            @pl.when(m > 0)
            def _():
                pltpu.make_async_copy(inbox.at[m], inbox.at[m], m_recv.at[m]).wait()

            @pl.loop(0, classes)
            def _(i):
                j = lax.rem(me + classes - i, classes)
                turned[strip(i), :] = inbox[m, strip(j), :].astype(F32).T

            second = partner_of(me, m, n_mom)

            @pl.loop(0, m + 1)
            def _(k):
                first = partner_of(me, k, n_mom)
                value = jnp.sum(inbox[k].astype(F32) * turned[...])
                hit = ((row == first) & (column == second)) | ((row == second) & (column == first))
                grid[...] += jnp.where(hit, value, 0.0)

    if_class(me, traces)

    g_sends = []
    for m in range(1, n_mom):
        send = pltpu.make_async_remote_copy(
            src_ref=grid, dst_ref=grids.at[m],
            send_sem=g_send.at[m], recv_sem=g_recv.at[m],
            device_id={"mom": partner_of(me, m, n_mom)},
            device_id_type=pl.DeviceIdType.MESH,
        )
        send.start()
        g_sends.append(send)
    total = grid[...]
    for m, send in zip(range(1, n_mom), g_sends):
        send.wait_recv()
        total = total + grids[m]

    line = lax.broadcasted_iota(jnp.int32, (diag_count, LANES), 0)
    picked = jnp.zeros((diag_count, LANES), F32)
    for d in range(diag_count):
        first = diag_ref[me * diag_count + d, 0]
        second = diag_ref[me * diag_count + d, 1]
        value = jnp.sum(jnp.where((row == first) & (column == second), total, 0.0))
        picked = jnp.where(line == d, value, picked)
    corr_ref[...] = picked[:, :1] / order

    for send in sends + g_sends:
        send.wait_send()
    if square:
        for c in range(n_chunk):
            forward(1 if c < n_chunk // 2 else 2, c).wait_send()
    for m in far_first:
        if_class(partner_of(me, m, n_mom), lambda: post(m).wait_send())
    out_copy.wait()


def body(n_t, n_mom, perambulators, elementals, src_times, diagrams):
    n_src, order = perambulators.shape[1], perambulators.shape[2]
    classes = order // LANES
    diag_count = diagrams.shape[0] // n_mom
    n_chunk = order // CHUNK
    meson, correlators = pl.pallas_call(
        functools.partial(kernel, n_t, n_mom, n_src, classes, diag_count),
        out_shape=(
            jax.ShapeDtypeStruct((order, order), BF16),
            jax.ShapeDtypeStruct((diag_count, 1), F32),
        ),
        in_specs=[
            pl.BlockSpec(memory_space=pltpu.SMEM),
            pl.BlockSpec(memory_space=pltpu.SMEM),
            pl.BlockSpec(memory_space=pl.ANY),
            pl.BlockSpec(memory_space=pl.ANY),
        ],
        out_specs=(
            pl.BlockSpec(memory_space=pl.ANY),
            pl.BlockSpec(memory_space=pltpu.VMEM),
        ),
        scratch_shapes=[
            pltpu.VMEM((n_src, order, order), BF16),
            pltpu.VMEM((n_t, order, order), BF16),
            pltpu.VMEM((order, order), F32),
            pltpu.VMEM((CHUNK, order), BF16),
            pltpu.VMEM((order, order), BF16),
            pltpu.VMEM((classes, order, LANES), BF16),
            pltpu.VMEM((n_mom, order, LANES), BF16),
            pltpu.VMEM((order, LANES), F32),
            pltpu.VMEM((n_mom, LANES), F32),
            pltpu.VMEM((n_mom, n_mom, LANES), F32),
            pltpu.SemaphoreType.DMA((n_src,)),
            pltpu.SemaphoreType.DMA((n_t, n_chunk)),
            pltpu.SemaphoreType.DMA((n_chunk,)),
            pltpu.SemaphoreType.DMA((n_t, n_chunk)),
            pltpu.SemaphoreType.DMA,
            pltpu.SemaphoreType.DMA((n_mom,)),
            pltpu.SemaphoreType.DMA((n_mom,)),
            pltpu.SemaphoreType.DMA((n_mom,)),
            pltpu.SemaphoreType.DMA((n_mom,)),
        ],
        compiler_params=pltpu.CompilerParams(
            collective_id=0, has_side_effects=True, vmem_limit_bytes=56 * 1024 * 1024
        ),
        cost_estimate=pl.CostEstimate(
            flops=4 * n_src * order ** 3, bytes_accessed=12 * order * order * 2, transcendentals=0
        ),
    )(src_times, diagrams, perambulators[0], elementals[0, 0])
    return meson[None, None], correlators


def solution(mesh):
    in_specs = (P("tsink", None, None, None), P("tsink", "mom", None, None), P(), P())
    out_specs = (P("tsink", "mom", None, None), P("mom", "tsink"))
    run = functools.partial(body, mesh.shape["tsink"], mesh.shape["mom"])
    return jax.shard_map(run, mesh=mesh, in_specs=in_specs, out_specs=out_specs, check_vma=False)
```

time: 568 us -> 141 us (0.25)
  waiting for transfers between devices: 324 us -> 0 us
  Pallas kernels: 0 us -> 135 us
  other arithmetic: 74.2 us -> 0 us
  local copies, waits for them, and re-layouts: 77.6 us -> 5.72 us
  matrix products: 39.5 us -> 0 us
  loops' own time: 34.1 us -> 0 us
  between operations: 16.6 us -> 0.64 us
    psum x1 -> x0, waiting for transfers between devices: 176 us -> none  [from_root(): return lax.psum(block, axis)]
    all_gather x1 -> x0, waiting for transfers between devices: 148 us -> none  [body(): gathered = lax.all_gather(meson[None], 'mom', axis=0, tiled=True)]
    pallas_call x0 -> x1, Pallas kernels: none -> 135 us  [body(): pl.pallas_call(functools.partial(kernel, n_t, n_mom, n_src, classes, diag...]
    while x9 -> x0, local copies, waits for them, and re-layouts: 65.3 us -> none
    dot_general x4 -> x0, matrix products: 39.5 us -> none  [body(): jnp.dot(propagators[source], half_product, preferred_element_type=jnp.flo...]
    dot_general x8 -> x0, other arithmetic: 36.9 us -> none  [whole_trace(): jnp.einsum('ij,ji->', gathered[diagram_pair[0]], gathered[diagram_pair[1]...]
    another operation x1 -> x0, loops' own time: 34.1 us -> none  [body(): traces = lax.map(whole_trace, own_diagrams)]
    while x8 -> x0, other arithmetic: 32.2 us -> none
  transfers between devices with their start and end apart: 2 -> 0, of which waited for: 2 -> 0; matrix products, arithmetic and copies ran while one was open for 0% -> 0% of each run, Pallas kernels for 0% -> 0%
where the time goes in v1:
time: 141 us
  Pallas kernels  135 us (96%)
  local copies, waits for them, and re-layouts  5.72 us (4%)
    pallas_call x1, Pallas kernels, body(): pl.pallas_call(functools.partial(kernel, n_t, n_mom, n_src, classes, diag...  135 us
    unnamed x3, local copies, waits for them, and re-layouts  5.72 us

profile of v1, /device:TPU:0, one launch (start us, length us, event | category | flops | bytes accessed | tf_op | source)
XLA Modules:
  0.0 141.2 jit_solution(4343905375266533537)
XLA Ops:
  0.6 1.4 copy.6.diag_ref
  2.0 134.8 %shard_map.59 = (bf16[1024,1024]{1,0:T(8,128)(2,1)}, f32[8,1]{1,0:T(8,128)}) custom-call(s32[4]{0:T(128)} %src_ref.1, s32[64,2]{1,0:T(8,128)} %copy.6.diag_ref, bf16[4,1024,1024]{2,1,0:T(8,128)(2,1)} %bitcast.4, bf16[1024,1024]{1,0:T(8,128)(2,1)} %bitcast.5), custom_call_target="tpu_custom_call" | custom-call | flops 17179869184 | bytes 25165824 | tf_op jit(solution)/shard_map/pallas_call | solution.py:255
  136.8 1.3 copy.7
  138.1 3.1 %copy.9 = bf16[1,1,1024,1024]{3,2,1,0:T(8,128)(2,1)} copy(bf16[1,1,1024,1024]{3,2,1,0:T(8,128)(2,1)} %bitcast.3) | data formatting | bytes 4194304

commit v2 on v1

v2 whole, which is shorter than its diff:
```python
import functools

import jax
import jax.numpy as jnp
from jax import lax
from jax.experimental import pallas as pl
from jax.experimental.pallas import tpu as pltpu
from jax.sharding import PartitionSpec as P

LANES = 128
CHUNK = 256
UNROLL = True
EARLY = 1
BF16 = jnp.bfloat16
F32 = jnp.float32


def partner_of(index, mask, size):
    out, digit = 0, 1
    while digit < size:
        mine = lax.rem(lax.div(index, digit), 2)
        if isinstance(mask, int):
            other = (mask // digit) % 2
        else:
            other = lax.rem(lax.div(mask, digit), 2)
        out = out + digit * lax.rem(mine + other, 2)
        digit *= 2
    return out


def kernel(
    n_t, n_mom, n_src, classes, diag_count,
    src_ref, diag_ref, p_hbm, e_hbm,
    meson_ref, corr_ref,
    p, e, acc, half, outbox, inbox, turned, pairs, grid, grids,
    p_sem, e_send, e_fwd, e_recv, turn, m_send, m_recv, g_send, g_recv,
):
    order = p.shape[1]
    n_chunk = order // CHUNK
    t = lax.axis_index("tsink")
    me = lax.axis_index("mom")

    def rows(c):
        return pl.ds(pl.multiple_of(c * CHUNK, CHUNK), CHUNK)

    p_copies = [
        pltpu.make_async_copy(p_hbm.at[s], p.at[s], p_sem.at[s]) for s in range(n_src)
    ]
    own_copies = [
        pltpu.make_async_copy(
            e_hbm.at[pl.ds(c * CHUNK, CHUNK)], e.at[0, pl.ds(c * CHUNK, CHUNK)], e_recv.at[0, c]
        )
        for c in range(n_chunk)
    ]
    for copy in p_copies + own_copies:
        copy.start()

    barrier = pltpu.get_barrier_semaphore()
    for m in range(1, n_t):
        pl.semaphore_signal(
            barrier, inc=1, device_id={"tsink": partner_of(t, m, n_t)},
            device_id_type=pl.DeviceIdType.MESH,
        )
    for m in range(1, n_mom):
        pl.semaphore_signal(
            barrier, inc=1, device_id={"mom": partner_of(me, m, n_mom)},
            device_id_type=pl.DeviceIdType.MESH,
        )
    pl.semaphore_wait(barrier, n_t - 1 + n_mom - 1)

    square = n_t == 4
    direct = (1, 2) if square else tuple(range(1, n_t))
    sends = []
    for k in range(n_chunk):
        for m in direct:
            c = (k + n_chunk // 2) % n_chunk if square and m == 2 else k
            part = pl.ds(c * CHUNK, CHUNK)
            sends.append(
                pltpu.make_async_remote_copy(
                    src_ref=e_hbm.at[part], dst_ref=e.at[m, part],
                    send_sem=e_send.at[m, c], recv_sem=e_recv.at[m, c],
                    device_id={"tsink": partner_of(t, m, n_t)},
                    device_id_type=pl.DeviceIdType.MESH,
                )
            )

    def start_sends():
        for send in sends:
            send.start()

    even = lax.rem(me, 2) == 0
    pl.when(even)(start_sends)

    def forward(slot, c):
        return pltpu.make_async_remote_copy(
            src_ref=e.at[slot, rows(c)], dst_ref=e.at[3, rows(c)],
            send_sem=e_fwd.at[c], recv_sem=e_recv.at[3, c],
            device_id={"tsink": partner_of(t, 3 - slot, n_t)},
            device_id_type=pl.DeviceIdType.MESH,
        )

    def arrived(slot, c):
        pltpu.make_async_copy(e.at[slot, rows(c)], e.at[slot, rows(c)], e_recv.at[slot, c]).wait()

    acc[...] = jnp.zeros_like(acc)
    for copy in p_copies:
        copy.wait()

    def source_of(slot):
        time = partner_of(t, slot, n_t)
        source = jnp.int32(0)
        weight = jnp.float32(0)
        for s in range(n_src):
            hit = src_ref[s] == time
            source = jnp.where(hit, jnp.int32(s), source)
            weight = jnp.where(hit, jnp.float32(1), weight)
        return source, weight

    def half_chunk(slot, c, place):
        source, weight = source_of(slot)
        chunk = e[slot, rows(c), :]

        @pl.loop(0, order // CHUNK, unroll=UNROLL)
        def _(n):
            product = lax.dot_general(
                chunk, p[source, rows(n), :], (((1,), (1,)), ((), ())),
                preferred_element_type=F32,
            )
            if n_t > n_src:
                product = product * weight
            half[place, :, rows(n)] = product.astype(BF16)

    def add_chunk(slot, c):
        half_chunk(slot, c, 0)
        source, _ = source_of(slot)

        @pl.loop(0, order // CHUNK, unroll=UNROLL)
        def _(n):
            acc[rows(n), :] += jnp.dot(
                p[source, rows(n), rows(c)], half[0], preferred_element_type=F32
            )

    def step_of(k):
        slot, c = lax.div(k, n_chunk), lax.rem(k, n_chunk)
        if not square:
            return slot, c
        shift = n_chunk // 2
        near = (slot == 1) | (slot == 2)
        near_c = lax.rem(lax.div(k - n_chunk, 2) + lax.rem(k, 2) * shift, n_chunk)
        far_c = lax.div(c, 2) + lax.rem(c, 2) * shift
        slot = jnp.where(near, 1 + lax.rem(k, 2), slot)
        return slot, jnp.where(near, near_c, jnp.where(slot == 3, far_c, c))

    last = n_t * n_chunk - 2

    @pl.loop(0, last)
    def _(k):
        @pl.when((k == n_chunk) & jnp.logical_not(even))
        def _():
            pl.semaphore_wait(turn, 1)
            start_sends()

        slot, c = step_of(k)
        arrived(slot, c)
        if square:
            @pl.when((k >= n_chunk) & (k < 2 * n_chunk))
            def _():
                forward(slot, c).start()

        @pl.when((k == last - EARLY) & even)
        def _():
            pl.semaphore_signal(
                turn, inc=1, device_id={"mom": partner_of(me, 1, n_mom)},
                device_id_type=pl.DeviceIdType.MESH,
            )

        add_chunk(slot, c)

    def strip(i):
        return pl.ds(pl.multiple_of(i * LANES, LANES), LANES)

    def post(m, n):
        to = partner_of(me, m, n_mom)
        return pltpu.make_async_remote_copy(
            src_ref=outbox.at[lax.rem(to, classes), rows(n)], dst_ref=inbox.at[m, rows(n)],
            send_sem=m_send.at[m, n], recv_sem=m_recv.at[m, n],
            device_id={"mom": to}, device_id_type=pl.DeviceIdType.MESH,
        )

    def if_class(index, action):
        if classes == n_mom:
            action()
        else:
            pl.when(index < classes)(action)

    far_first = sorted(range(1, n_mom), key=lambda m: -(m // (n_mom // 2)))

    for place in range(2):
        slot, c = step_of(jnp.int32(last + place))
        arrived(slot, c)
        half_chunk(slot, c, place)
    source, _ = source_of(slot)
    columns = [rows(step_of(jnp.int32(last + place))[1]) for place in range(2)]

    @pl.loop(0, n_chunk)
    def _(n):
        values = acc[rows(n), :]
        for place in range(2):
            values = values + jnp.dot(
                p[source, rows(n), columns[place]], half[place], preferred_element_type=F32
            )
        values = values.astype(BF16)
        meson_ref[rows(n), :] = values
        for r in range(CHUNK // LANES):
            i = n * (CHUNK // LANES) + r
            for j in range(classes):
                outbox[lax.rem(i + j, classes), strip(i), :] = values[
                    r * LANES:(r + 1) * LANES, j * LANES:(j + 1) * LANES
                ]
        for m in far_first:
            if_class(partner_of(me, m, n_mom), lambda: post(m, n).start())


    row = lax.broadcasted_iota(jnp.int32, grid.shape, 0)
    column = lax.broadcasted_iota(jnp.int32, grid.shape, 1)
    pairs[...] = jnp.zeros_like(pairs)

    def traces():
        inbox[0] = outbox[lax.rem(me, classes)]

        @pl.loop(0, n_mom)
        def _(m):
            @pl.when(m > 0)
            def _():
                for n in range(n_chunk):
                    part = inbox.at[m, rows(n)]
                    pltpu.make_async_copy(part, part, m_recv.at[m, n]).wait()

            @pl.loop(0, classes, unroll=UNROLL)
            def _(i):
                j = lax.rem(me + classes - i, classes)
                turned[strip(i), :] = inbox[m, strip(j), :].astype(F32).T

            second = partner_of(me, m, n_mom)

            @pl.loop(0, m + 1)
            def _(k):
                first = partner_of(me, k, n_mom)
                pairs[second, pl.ds(first, 1), :] = jnp.sum(
                    inbox[k].astype(F32) * turned[...], axis=0, keepdims=True
                )

    if_class(me, traces)

    own = jnp.zeros_like(grid)
    for q in range(n_mom):
        own = jnp.where(column == q, jnp.sum(pairs[q], axis=1, keepdims=True), own)
    grid[...] = own

    g_sends = []
    for m in range(1, n_mom):
        send = pltpu.make_async_remote_copy(
            src_ref=grid, dst_ref=grids.at[m],
            send_sem=g_send.at[m], recv_sem=g_recv.at[m],
            device_id={"mom": partner_of(me, m, n_mom)},
            device_id_type=pl.DeviceIdType.MESH,
        )
        send.start()
        g_sends.append(send)
    total = grid[...]
    for m, send in zip(range(1, n_mom), g_sends):
        send.wait_recv()
        total = total + grids[m]

    line = lax.broadcasted_iota(jnp.int32, (diag_count, LANES), 0)
    lane = lax.broadcasted_iota(jnp.int32, (diag_count, LANES), 1)
    picked = jnp.zeros((diag_count, LANES), F32)
    for d in range(diag_count):
        first = diag_ref[0, me * diag_count + d]
        second = diag_ref[1, me * diag_count + d]
        hit = ((row == first) & (column == second)) | ((row == second) & (column == first))
        value = jnp.sum(jnp.where(hit, total, 0.0), axis=0, keepdims=True)
        picked = jnp.where(line == d, value, picked)
    picked = jnp.sum(picked, axis=1, keepdims=True) / order
    corr_ref[...] = jnp.sum(jnp.where(line == lane, picked, 0.0), axis=0, keepdims=True)[:, :diag_count]

    for send in sends + g_sends:
        send.wait_send()
    if square:
        for c in range(n_chunk):
            forward(1 if c < n_chunk // 2 else 2, c).wait_send()
    for m in far_first:
        if_class(partner_of(me, m, n_mom), lambda: pl.loop(0, n_chunk)(lambda n: post(m, n).wait_send()))


def body(n_t, n_mom, perambulators, elementals, src_times, diagrams):
    n_src, order = perambulators.shape[1], perambulators.shape[2]
    classes = order // LANES
    diag_count = diagrams.shape[0] // n_mom
    n_chunk = order // CHUNK
    meson, correlators = pl.pallas_call(
        functools.partial(kernel, n_t, n_mom, n_src, classes, diag_count),
        out_shape=(
            pltpu.VMEM((order, order), BF16),
            jax.ShapeDtypeStruct((1, diag_count), F32),
        ),
        in_specs=[
            pl.BlockSpec(memory_space=pltpu.SMEM),
            pl.BlockSpec(memory_space=pltpu.SMEM),
            pl.BlockSpec(memory_space=pl.ANY),
            pl.BlockSpec(memory_space=pl.ANY),
        ],
        out_specs=(
            pl.BlockSpec(memory_space=pltpu.VMEM),
            pl.BlockSpec(memory_space=pltpu.VMEM),
        ),
        scratch_shapes=[
            pltpu.VMEM((n_src, order, order), BF16),
            pltpu.VMEM((n_t, order, order), BF16),
            pltpu.VMEM((order, order), F32),
            pltpu.VMEM((2, CHUNK, order), BF16),
            pltpu.VMEM((classes, order, LANES), BF16),
            pltpu.VMEM((n_mom, order, LANES), BF16),
            pltpu.VMEM((order, LANES), F32),
            pltpu.VMEM((n_mom, n_mom, LANES), F32),
            pltpu.VMEM((n_mom, LANES), F32),
            pltpu.VMEM((n_mom, n_mom, LANES), F32),
            pltpu.SemaphoreType.DMA((n_src,)),
            pltpu.SemaphoreType.DMA((n_t, n_chunk)),
            pltpu.SemaphoreType.DMA((n_chunk,)),
            pltpu.SemaphoreType.DMA((n_t, n_chunk)),
            pltpu.SemaphoreType.REGULAR,
            pltpu.SemaphoreType.DMA((n_mom, n_chunk)),
            pltpu.SemaphoreType.DMA((n_mom, n_chunk)),
            pltpu.SemaphoreType.DMA((n_mom,)),
            pltpu.SemaphoreType.DMA((n_mom,)),
        ],
        compiler_params=pltpu.CompilerParams(
            collective_id=0, has_side_effects=True, vmem_limit_bytes=50 * 1024 * 1024
        ),
        cost_estimate=pl.CostEstimate(
            flops=4 * n_src * order ** 3, bytes_accessed=12 * order * order * 2, transcendentals=0
        ),
    )(src_times, diagrams.T, perambulators[0], elementals[0, 0])
    return meson[None, None], correlators.T


def solution(mesh):
    in_specs = (P("tsink", None, None, None), P("tsink", "mom", None, None), P(), P())
    out_specs = (P("tsink", "mom", None, None), P("mom", "tsink"))
    run = functools.partial(body, mesh.shape["tsink"], mesh.shape["mom"])
    return jax.shard_map(run, mesh=mesh, in_specs=in_specs, out_specs=out_specs, check_vma=False)
```

time: 141 us -> 114 us (0.81)
  Pallas kernels: 135 us -> 110 us
  local copies, waits for them, and re-layouts: 5.72 us -> 3.16 us
    pallas_call x1, Pallas kernels: 135 us -> 110 us  [body(): pl.pallas_call(functools.partial(kernel, n_t, n_mom, n_src, classes, diag...]
    unnamed x3 -> x6, local copies, waits for them, and re-layouts: 5.72 us -> 3.16 us
where the time goes in v2:
time: 114 us
  Pallas kernels  110 us (96%)
  local copies, waits for them, and re-layouts  3.16 us (3%)
    pallas_call x1, Pallas kernels, body(): pl.pallas_call(functools.partial(kernel, n_t, n_mom, n_src, classes, diag...  110 us
    unnamed x6, local copies, waits for them, and re-layouts  3.16 us

profile of v2, /device:TPU:0, one launch (start us, length us, event | category | flops | bytes accessed | tf_op | source)
XLA Modules:
  0.0 113.5 jit_solution(2258476062956958678)
XLA Ops:
  0.6 0.0 copy-start
  0.6 0.7 copy-done
  1.3 0.0 copy-start.1
  1.3 0.7 copy-done.1
  2.0 109.7 %shard_map.59 = (bf16[1024,1024]{1,0:T(8,128)(2,1)S(1)}, f32[1,8]{1,0:T(1,128)S(1)}) custom-call(s32[4]{0:T(128)S(1)} %copy-done.1, s32[2,64]{1,0:T(2,128)S(1)} %bitcast.6, bf16[4,1024,1024]{2,1,0:T(8,128)(2,1)} %bitcast.8, bf16[1024,1024]{1,0:T(8,128)(2,1)} %bitcast.9), custom_call_target="tpu_custom_call" | custom-call | flops 17179869184 | bytes 25165824 | tf_op jit(solution)/shard_map/pallas_call | solution.py:301
  111.7 1.3 %copy.8 = bf16[1,1,1024,1024]{3,2,1,0:T(8,128)(2,1)} copy(bf16[1,1,1024,1024]{3,2,1,0:T(8,128)(2,1)S(1)} %bitcast.5) | data formatting | bytes 4194304
  113.0 0.5 copy.9
Async XLA Ops:
  0.6 0.7 copy-start
  1.3 0.7 copy-start.1

commit v3 on v2

--- a/solution.py
+++ b/solution.py
@@ -228,8 +228,14 @@
     def traces():
         inbox[0] = outbox[lax.rem(me, classes)]
 
+        def in_order(position):
+            group = lax.div(position, n_mom // 2) + lax.rem(me, 2)
+            return 2 * lax.rem(position, n_mom // 2) + lax.rem(group, 2)
+
         @pl.loop(0, n_mom)
-        def _(m):
+        def _(position):
+            m = in_order(position)
+
             @pl.when(m > 0)
             def _():
                 for n in range(n_chunk):
@@ -243,8 +249,9 @@
 
             second = partner_of(me, m, n_mom)
 
-            @pl.loop(0, m + 1)
-            def _(k):
+            @pl.loop(0, position + 1)
+            def _(earlier):
+                k = in_order(earlier)
                 first = partner_of(me, k, n_mom)
                 pairs[second, pl.ds(first, 1), :] = jnp.sum(
                     inbox[k].astype(F32) * turned[...], axis=0, keepdims=True

time: 114 us -> 113 us (level)
  no operation moved by 1% of the time
where the time goes in v3:
time: 113 us
  Pallas kernels  109 us (96%)
  local copies, waits for them, and re-layouts  3.16 us (3%)
    pallas_call x1, Pallas kernels, body(): pl.pallas_call(functools.partial(kernel, n_t, n_mom, n_src, classes, diag...  109 us
    unnamed x6, local copies, waits for them, and re-layouts  3.16 us

profile of v3, /device:TPU:0, one launch (start us, length us, event | category | flops | bytes accessed | tf_op | source)
XLA Modules:
  0.0 112.6 jit_solution(11159387667397209476)
XLA Ops:
  0.6 0.0 copy-start
  0.6 0.7 copy-done
  1.3 0.0 copy-start.1
  1.3 0.7 copy-done.1
  2.0 108.8 %shard_map.59 = (bf16[1024,1024]{1,0:T(8,128)(2,1)S(1)}, f32[1,8]{1,0:T(1,128)S(1)}) custom-call(s32[4]{0:T(128)S(1)} %copy-done.1, s32[2,64]{1,0:T(2,128)S(1)} %bitcast.6, bf16[4,1024,1024]{2,1,0:T(8,128)(2,1)} %bitcast.8, bf16[1024,1024]{1,0:T(8,128)(2,1)} %bitcast.9), custom_call_target="tpu_custom_call" | custom-call | flops 17179869184 | bytes 25165824 | tf_op jit(solution)/shard_map/pallas_call | solution.py:308
  110.7 1.3 %copy.8 = bf16[1,1,1024,1024]{3,2,1,0:T(8,128)(2,1)} copy(bf16[1,1,1024,1024]{3,2,1,0:T(8,128)(2,1)S(1)} %bitcast.5) | data formatting | bytes 4194304
  112.1 0.5 copy.9
Async XLA Ops:
  0.6 0.7 copy-start
  1.3 0.7 copy-start.1
